TPU v7x, 256 devices: a whole 4x4x8 slice. The times are simulated.
256 devices in a mesh: expert: 64 (over z, x, core), zero: 4 (over y).
Axes of the slice: x: 4, y: 4, z: 8, core: 2. Of those that a mesh axis runs over, the one named last changes fastest.
Arguments:
- cotangent: bfloat16 [32768, 2048], P(('expert', 'zero')), may hold values from -0.59765625 to 0.59765625
- gates: float32 [32768, 8], P(('expert', 'zero')), may hold values from 0.05 to 1
- expert_ids: int32 [32768, 8], P(('expert', 'zero')), may hold values from 0 to 127, all different within a row; in each aligned block of 128 rows (0 to 127, 128 to 255, ...) at most 16 rows name the same one
- hidden: bfloat16 [128, 4096, 768], P('expert', 'zero'), may hold values from -6 to 6
- momentum_left: float32 [128, 768, 32], P('expert', 'zero'), may hold values from -6 to 6
- momentum_right: float32 [128, 32, 2048], P('expert', None, 'zero'), may hold values from -1 to 1
- sketch: float32 [128, 2048, 32], P('expert'), may hold values from -6 to 6
Outputs:
- basis: float32 [128, 768, 32], P('expert', 'zero')
- coefficients: float32 [128, 32, 2048], P('expert', None, 'zero')
Inputs may be any that keep to these rules, and one draw needn't show every extreme that they name: `expert_ids`: among the 128 tokens of one device (an aligned block of rows) no expert is named more than 16 times, a bound that some block reaches; the 8 experts of a token differ.
All inputs are finite; a program needn't handle non-finite values.
Results may differ from a plain program's by a relative error of at most 0.0035.
Values may be sent and summed in bfloat16 or wider, within the bound.
No kernel may reach another device: no remote copies, remote signals or barrier semaphores. Data moves between devices by JAX's collectives and lax.ppermute only.
A program may use at most 128 MiB of HBM per device.

v0:
```python
import jax
import jax.numpy as jnp
from jax import lax
from jax.sharding import PartitionSpec as P

FF = 768
CAP = 16
MOMENTUM_DECAY = 0.9


def slot_table(ids_block, count):
    flat = ids_block.reshape(-1)
    onehot = (flat[:, None] == jnp.arange(count, dtype=jnp.int32)[None, :]).astype(jnp.int32)
    before = jnp.cumsum(onehot, axis=0) - onehot
    return jnp.sum(before * onehot, axis=1)


def orthonormal(rows_y):
    highest = lax.Precision.HIGHEST
    local_gram = jnp.einsum("efr,efs->ers", rows_y, rows_y, precision=highest)
    gram = lax.psum(local_gram, "zero") / FF
    lower = jnp.linalg.cholesky(gram)
    basis_t = lax.linalg.triangular_solve(
        lower, jnp.swapaxes(rows_y, 1, 2), left_side=True, lower=True
    )
    return jnp.swapaxes(basis_t, 1, 2)


def body(cotangent, gates, expert_ids, hidden, momentum_left, momentum_right, sketch):
    highest = lax.Precision.HIGHEST
    local_experts = hidden.shape[0]
    experts = local_experts * lax.axis_size("expert")
    width = cotangent.shape[1]
    slots = slot_table(expert_ids, experts)
    scaled = (gates[:, :, None] * cotangent[:, None, :].astype(jnp.float32)).astype(jnp.bfloat16)
    target = expert_ids.reshape(-1) * CAP + slots
    outgoing = (
        jnp.zeros((experts * CAP, width), jnp.bfloat16).at[target].set(scaled.reshape(-1, width))
    )
    outgoing = outgoing.reshape(experts, CAP, width)
    arrived = lax.all_to_all(outgoing, "expert", split_axis=0, concat_axis=1, tiled=True)
    right_full = lax.all_gather(momentum_right, "zero", axis=2, tiled=True)
    grad_local = jnp.transpose(
        lax.psum_scatter(
            jnp.einsum("esf,esd->fed", hidden, arrived, preferred_element_type=jnp.float32),
            "zero",
            scatter_dimension=0,
            tiled=True,
        ),
        (1, 0, 2),
    )
    merged = (
        MOMENTUM_DECAY * jnp.einsum("efr,erd->efd", momentum_left, right_full, precision=highest)
        + grad_local
    )
    sketched = jnp.einsum("efd,edr->efr", merged, sketch, precision=highest)
    basis = orthonormal(sketched)
    coeff_part = jnp.einsum("efr,efd->erd", basis, merged, precision=highest) / FF
    coefficients = lax.psum_scatter(coeff_part, "zero", scatter_dimension=2, tiled=True)
    return (basis, coefficients)


def solution(mesh):
    return jax.shard_map(
        body,
        mesh=mesh,
        in_specs=(
            P(("expert", "zero"), None),
            P(("expert", "zero"), None),
            P(("expert", "zero"), None),
            P("expert", "zero", None),
            P("expert", "zero", None),
            P("expert", None, "zero"),
            P("expert", None, None),
        ),
        out_specs=(P("expert", "zero", None), P("expert", None, "zero")),
        check_vma=False,
    )
```

profile of v0, /device:TPU:4, one launch (start us, length us, event | category | flops | bytes accessed | tf_op | source)
XLA Modules:
  0.0 433.0 jit_solution(7528596243765966278)
XLA Ops:
  7.2 0.0 copy-start
  7.2 0.0 copy-start.7
  7.2 0.0 reduce-scatter.3.cloned.1.call-start
  7.2 0.9 copy.26
  8.2 0.1 eq.29
  8.3 0.1 eq.25
  8.4 0.7 broadcast_multiply_fusion.1
  9.0 0.1 copy.28
  9.2 0.2 fusion.8
  9.4 0.0 copy-start.2
  9.4 0.8 copy-done.2
  10.2 1.1 broadcast_add_fusion
  11.3 0.9 copy.29
  12.1 0.1 copy.25
  12.2 0.1 mul.47
  12.3 2.2 convert_element_type.17
  14.6 0.0 copy-done.7
  14.6 0.1 copy.30
  14.7 0.1 mul.49
  14.8 1.4 fusion.7
  16.2 12.1 %scatter_custom_fusion = bf16[2048,2048]{1,0:T(8,128)(2,1)} fusion(s32[1024]{0:T(1024)S(1)} %bitcast.52, f32[128,2048]{1,0:T(8,128)} %convert_element_type.17, f32[1024]{0:T(1024)S(1)} %mul.49, bf16[]{:T(256)} %constant.54.clone.1), kind=kCustom, calls=%fused_computation.4 | custom fusion | flops 4194304 | bytes 9441282 | tf_op jit(solution)/shard_map/scatter | solution.py:38
  28.3 198.2 %all_to_all.18 = bf16[128,16,2048]{2,1,0:T(8,128)(2,1)} all-to-all(bf16[128,16,2048]{2,1,0:T(8,128)(2,1)} %bitcast.47), channel_id=1, replica_groups=mesh['expert'=64,'zero'=4] {'expert'}, dimensions={0} | all-to-all | bytes 16777216 | tf_op jit(solution)/shard_map/all_to_all | solution.py:41
  226.4 8.3 %copy.31 = bf16[2,64,16,2048]{3,2,1,0:T(8,128)(2,1)} copy(bf16[2,64,16,2048]{3,2,0,1:T(8,128)(2,1)} %bitcast.48) | data formatting | bytes 16777216 | tf_op jit(solution)/shard_map/all_to_all | solution.py:41
  234.7 0.0 copy-done
  234.7 12.6 %convolution_bitcast_fusion = f32[768,2,2048]{2,0,1:T(8,128)} fusion(bf16[2,1024,2048]{2,1,0:T(8,128)(2,1)} %bitcast.49, bf16[2,1024,768]{2,1,0:T(8,128)(2,1)S(1)} %copy-done), kind=kOutput, calls=%fused_computation.3 | convolution fusion | flops 6442450944 | bytes 24117248 | tf_op jit(solution)/shard_map/esf,esd->fed/dot_general | solution.py:45
  247.3 0.0 copy-start.5
  247.3 0.0 copy-start.6
  247.3 0.0 reduce-scatter.3.cloned.1.call-update
  247.3 0.0 reduce-scatter.5.cloned.1.call-start
  247.4 0.8 copy-done.5
  248.2 15.8 %all_gather.3 = f32[2,32,2048]{2,1,0:T(8,128)} all-gather(f32[2,32,512]{2,1,0:T(8,128)S(1)} %copy-done.5), channel_id=1, replica_groups=mesh['expert'=64,'zero'=4] {'zero'}, dimensions={2}, use_global_device_ids=true | all-gather | bytes 655360 | tf_op jit(solution)/shard_map/all_gather | solution.py:42
  264.0 98.7 %reduce-scatter.3.cloned.1.call-done = f32[192,2,2048]{2,0,1:T(8,128)} async-done(((f32[768,2,2048]{2,0,1:T(8,128)}), f32[192,2,2048]{2,0,1:T(8,128)}) %reduce-scatter.3.cloned.1.call-update) | async-done | bytes 3145744 | tf_op jit(solution)/shard_map/reduce_scatter | solution.py:44
  362.8 0.0 copy-done.6
  362.8 0.0 copy-start.3
  362.8 4.9 %bitcast_add_fusion = f32[2,192,2048]{2,1,0:T(8,128)S(1)} fusion(f32[192,2,2048]{2,0,1:T(8,128)} %reduce-scatter.3.cloned.1.call-done, f32[2,192,32]{1,2,0:T(8,128)S(1)} %copy-done.6, f32[2,32,2048]{2,1,0:T(8,128)} %all_gather.3), kind=kOutput, calls=%fused_computation.8 | convolution fusion | flops 303562752 | bytes 6864896 | tf_op jit(solution)/shard_map/efr,erd->efd/dot_general | solution.py:53
  367.7 0.0 copy-start.1
  367.7 1.7 copy-done.1
  369.4 0.0 copy-done.3
  369.4 3.1 fusion.14
  372.5 0.2 fusion.15
  372.7 15.0 %psum.7 = f32[2,32,32]{1,2,0:T(8,128)S(1)} all-reduce(f32[2,32,32]{1,2,0:T(8,128)S(1)} %fusion.15), channel_id=1, replica_groups=mesh['expert'=64,'zero'=4] {'zero'}, use_global_device_ids=true, to_apply=%region_5.6 | all-reduce | flops 2048 | bytes 16384 | tf_op jit(solution)/shard_map/psum | solution.py:21
  387.7 0.1 copy.35
  387.8 5.9 %custom-call.7 = f32[2,32,32]{2,1,0:T(8,128)S(1)} custom-call(f32[2,32,32]{2,1,0:T(8,128)S(1)} %fusion.13), custom_call_target="Cholesky" | custom-call | tf_op jit(solution)/shard_map/jit(cholesky)/cholesky | solution.py:22
  393.7 0.1 compare_reduce_fusion
  393.8 0.1 select_bitcast_fusion
  393.9 4.9 %custom-call.8 = f32[2,1,32,32]{2,3,1,0:T(8,128)S(1)} custom-call(f32[2,1,32,32]{3,2,1,0:T(8,128)S(1)} %select_bitcast_fusion), custom_call_target="InvertDiagBlocksLowerTriangular" | custom-call | tf_op jit(solution)/shard_map/triangular_solve | solution.py:23
  398.8 0.3 fusion.11
  399.1 0.0 copy-start.4
  399.1 4.7 %convolution_multiply_fusion = f32[2,32,2048]{2,1,0:T(8,128)} fusion(f32[2,32,192]{2,1,0:T(8,128)S(1)} %fusion.11, f32[2,192,2048]{2,1,0:T(8,128)} %copy-done.1), kind=kOutput, calls=%fused_computation.9 | convolution fusion | flops 302120960 | bytes 3719168 | tf_op jit(solution)/shard_map/efr,efd->erd/dot_general | solution.py:58
  403.8 0.0 reduce-scatter.5.cloned.1.call-update
  403.8 22.3 %reduce-scatter.5.cloned.1.call-done = f32[2,32,512]{2,1,0:T(8,128)} async-done(((f32[2,32,2048]{2,1,0:T(8,128)}), f32[2,32,512]{2,1,0:T(8,128)}) %reduce-scatter.5.cloned.1.call-update) | async-done | bytes 131088 | tf_op jit(solution)/shard_map/reduce_scatter | solution.py:59
  426.2 0.0 copy-done.4
  (9 shorter events, 0.1 us)
Async XLA Ops:
  7.2 227.6 %copy-start = (bf16[2,1024,768]{2,1,0:T(8,128)(2,1)S(1)}, bf16[2,1024,768]{2,1,0:T(8,128)(2,1)}, u32[]{:S(2)}) copy-start(bf16[2,1024,768]{2,1,0:T(8,128)(2,1)} %param.10) | copy-start | bytes 9437188
  7.2 7.4 %copy-start.7 = (f32[128,8]{0,1:T(8,128)S(1)}, f32[128,8]{0,1:T(8,128)}, u32[]{:S(2)}) copy-start(f32[128,8]{0,1:T(8,128)} %param.8) | copy-start | bytes 12292
  7.2 355.6 %reduce-scatter.3.cloned.1.call-start = ((), (), s32[]{:S(2)}) async-start(), calls=%async_computation.3 | async-start | bytes 15728640 | tf_op jit(solution)/shard_map/reduce_scatter | solution.py:44
  9.4 0.8 copy-start.2
  247.3 0.9 copy-start.5
  247.3 115.5 %copy-start.6 = (f32[2,192,32]{1,2,0:T(8,128)S(1)}, f32[2,192,32]{1,2,0:T(8,128)}, u32[]{:S(2)}) copy-start(f32[2,192,32]{1,2,0:T(8,128)} %param.11) | copy-start | bytes 147460
  247.3 178.9 %reduce-scatter.5.cloned.1.call-start = ((), (), s32[]{:S(2)}) async-start(), calls=%async_computation.4 | async-start | bytes 655360 | tf_op jit(solution)/shard_map/reduce_scatter | solution.py:59
  362.8 6.6 %copy-start.3 = (f32[2,2048,32]{1,2,0:T(8,128)S(1)}, f32[2,2048,32]{1,2,0:T(8,128)}, u32[]{:S(2)}) copy-start(f32[2,2048,32]{1,2,0:T(8,128)} %param.13) | copy-start | bytes 1572868
  367.7 1.7 copy-start.1
  399.1 27.1 %copy-start.4 = (f32[2,32,192]{2,1,0:T(8,128)}, f32[2,32,192]{2,1,0:T(8,128)S(1)}, u32[]{:S(2)}) copy-start(f32[2,32,192]{2,1,0:T(8,128)S(1)} %fusion.11) | copy-start | bytes 147460
Sparse Core Ops, SparseCore 0:
  247.4 115.2 reduce-scatter.2
  404.0 22.1 reduce-scatter.4
where the time goes:
time: 433 us
  blocking collectives  229 us (53%)
  waiting for transfers between devices  121 us (28%)
  other arithmetic  28.7 us (7%)
  matrix products  25.8 us (6%)
  between operations  14.2 us (3%)
  local copies, waits for them, and re-layouts  14.1 us (3%)
    all_to_all x1, blocking collectives, body(): lax.all_to_all(outgoing, 'expert', split_axis=0, concat_axis=1, tiled=True)  198 us
    reduce_scatter x1, waiting for transfers between devices, body(): lax.psum_scatter(jnp.einsum('esf,esd->fed', hidden, arrived, preferred_el...  98.7 us
    reduce_scatter x1, waiting for transfers between devices, body(): lax.psum_scatter(coeff_part, 'zero', scatter_dimension=2, tiled=True)  22.3 us
    all_gather x1, blocking collectives, body(): right_full = lax.all_gather(momentum_right, 'zero', axis=2, tiled=True)  15.8 us
    psum x1, blocking collectives, orthonormal(): gram = lax.psum(local_gram, 'zero') / FF  15 us
    dot_general x1, matrix products, body(): jnp.einsum('esf,esd->fed', hidden, arrived, preferred_element_type=jnp.fl...  12.6 us
    scatter x1, other arithmetic, body(): jnp.zeros((experts * CAP, width), jnp.bfloat16).at[target]  12.1 us
  transfers between devices with their start and end apart: 2, of which 2 were waited for; matrix products, arithmetic and copies ran while one was open for 0% of the time, Pallas kernels for 0%

commit v1 on v0

--- a/solution.py
+++ b/solution.py
@@ -39,7 +39,15 @@
     )
     outgoing = outgoing.reshape(experts, CAP, width)
     arrived = lax.all_to_all(outgoing, "expert", split_axis=0, concat_axis=1, tiled=True)
-    right_full = lax.all_gather(momentum_right, "zero", axis=2, tiled=True)
+    ways, here, step = (lax.axis_size("zero"), lax.axis_index("zero"), momentum_right.shape[2])
+    line, have = (momentum_right, 1)
+    while have < ways:
+        line = jnp.concatenate(
+            [line, lax.ppermute(line, "zero", [(d, (d - have) % ways) for d in range(ways)])],
+            axis=2,
+        )
+        have = 2 * have
+    right_full = jnp.roll(line, here * step, axis=2)
     grad_local = jnp.transpose(
         lax.psum_scatter(
             jnp.einsum("esf,esd->fed", hidden, arrived, preferred_element_type=jnp.float32),

time: 433 us -> 437 us (level)
  blocking collectives: 229 us -> 214 us
  local copies, waits for them, and re-layouts: 14.1 us -> 20.1 us
  waiting for transfers between devices: 121 us -> 127 us
  starting transfers between devices: 0.08 us -> 5.72 us
    all_gather x1 -> x0, blocking collectives: 15.8 us -> none  [body(): right_full = lax.all_gather(momentum_right, 'zero', axis=2, tiled=True)]
    ppermute x0 -> x2, waiting for transfers between devices: none -> 12.7 us  [body(): lax.ppermute(line, 'zero', [(d, (d - have) % ways) for d in range(ways)])]
    reduce_scatter x1, waiting for transfers between devices: 98.7 us -> 92.1 us  [body(): lax.psum_scatter(jnp.einsum('esf,esd->fed', hidden, arrived, preferred_el...]
    ppermute x0 -> x2, starting transfers between devices: none -> 5.64 us  [body(): lax.ppermute(line, 'zero', [(d, (d - have) % ways) for d in range(ways)])]
  transfers between devices with their start and end apart: 2 -> 4, of which waited for: 2 -> 4; matrix products, arithmetic and copies ran while one was open for 0% -> 2% of each run, Pallas kernels for 0% -> 0%
where the time goes in v1:
time: 437 us
  blocking collectives  214 us (49%)
  waiting for transfers between devices  127 us (29%)
  other arithmetic  29.6 us (7%)
  matrix products  25.8 us (6%)
  local copies, waits for them, and re-layouts  20.1 us (5%)
  between operations  14.2 us (3%)
  starting transfers between devices  5.72 us (1%)
    all_to_all x1, blocking collectives, body(): lax.all_to_all(outgoing, 'expert', split_axis=0, concat_axis=1, tiled=True)  198 us
    reduce_scatter x1, waiting for transfers between devices, body(): lax.psum_scatter(jnp.einsum('esf,esd->fed', hidden, arrived, preferred_el...  92.1 us
    reduce_scatter x1, waiting for transfers between devices, body(): lax.psum_scatter(coeff_part, 'zero', scatter_dimension=2, tiled=True)  22.4 us
    psum x1, blocking collectives, orthonormal(): gram = lax.psum(local_gram, 'zero') / FF  15.9 us
    ppermute x2, waiting for transfers between devices, body(): lax.ppermute(line, 'zero', [(d, (d - have) % ways) for d in range(ways)])  12.7 us
    dot_general x1, matrix products, body(): jnp.einsum('esf,esd->fed', hidden, arrived, preferred_element_type=jnp.fl...  12.6 us
    scatter x1, other arithmetic, body(): jnp.zeros((experts * CAP, width), jnp.bfloat16).at[target]  12.1 us
  transfers between devices with their start and end apart: 4, of which 4 were waited for; matrix products, arithmetic and copies ran while one was open for 2% of the time, Pallas kernels for 0%

profile of v1, /device:TPU:4, one launch (start us, length us, event | category | flops | bytes accessed | tf_op | source)
XLA Modules:
  0.0 436.6 jit_solution(295096192944677044)
XLA Ops:
  7.2 0.0 copy-start
  7.2 0.0 copy-start.7
  7.2 0.0 reduce-scatter.3.cloned.1.call-start
  7.2 0.8 broadcast_multiply_fusion.1
  8.1 0.9 copy.26
  8.9 0.1 eq.32
  9.0 0.1 eq.28
  9.1 0.1 copy.25
  9.2 0.1 mul.55
  9.3 0.1 copy.28
  9.4 0.2 fusion.8
  9.6 0.0 copy-start.2
  9.6 0.8 copy-done.2
  10.5 1.1 broadcast_add_fusion
  11.5 0.9 copy.29
  12.4 2.2 convert_element_type.17
  14.6 0.0 copy-done.7
  14.6 0.1 copy.30
  14.7 0.1 mul.57
  14.8 1.4 fusion.7
  16.3 12.1 %scatter_custom_fusion = bf16[2048,2048]{1,0:T(8,128)(2,1)} fusion(s32[1024]{0:T(1024)S(1)} %bitcast.53, f32[128,2048]{1,0:T(8,128)} %convert_element_type.17, f32[1024]{0:T(1024)S(1)} %mul.57, bf16[]{:T(256)} %constant.82.clone.1), kind=kCustom, calls=%fused_computation.4 | custom fusion | flops 4194304 | bytes 9441282 | tf_op jit(solution)/shard_map/scatter | solution.py:38
  28.3 198.2 %all_to_all.18 = bf16[128,16,2048]{2,1,0:T(8,128)(2,1)} all-to-all(bf16[128,16,2048]{2,1,0:T(8,128)(2,1)} %bitcast.48), channel_id=1, replica_groups=mesh['expert'=64,'zero'=4] {'expert'}, dimensions={0} | all-to-all | bytes 16777216 | tf_op jit(solution)/shard_map/all_to_all | solution.py:41
  226.5 8.3 %copy.31 = bf16[2,64,16,2048]{3,2,1,0:T(8,128)(2,1)} copy(bf16[2,64,16,2048]{3,2,0,1:T(8,128)(2,1)} %bitcast.49) | data formatting | bytes 16777216 | tf_op jit(solution)/shard_map/all_to_all | solution.py:41
  234.8 0.0 copy-done
  234.8 12.6 %convolution_bitcast_fusion = f32[768,2,2048]{2,0,1:T(8,128)} fusion(bf16[2,1024,2048]{2,1,0:T(8,128)(2,1)} %bitcast.50, bf16[2,1024,768]{2,1,0:T(8,128)(2,1)S(1)} %copy-done), kind=kOutput, calls=%fused_computation.3 | convolution fusion | flops 6442450944 | bytes 24117248 | tf_op jit(solution)/shard_map/esf,esd->fed/dot_general | solution.py:53
  247.4 0.0 copy-start.3
  247.4 0.0 copy-start.6
  247.4 0.0 reduce-scatter.3.cloned.1.call-update
  247.4 0.0 reduce-scatter.5.cloned.1.call-start
  247.4 0.8 copy-done.3
  248.3 3.0 collective-permute-start
  251.3 2.5 collective-permute-done
  253.8 0.7 pad_maximum_fusion
  254.5 2.6 collective-permute-start.1
  257.1 0.7 constant_dynamic-update-slice_fusion.5
  257.8 0.7 constant_dynamic-update-slice_fusion.4
  258.5 10.2 %collective-permute-done.1 = f32[2,32,1024]{2,1,0:T(8,128)} collective-permute-done((f32[2,32,1024]{2,1,0:T(8,128)}, f32[2,32,1024]{2,1,0:T(8,128)}, u32[]{:S(2)}, u32[]{:S(2)}) %collective-permute-start.1) | collective-permute-done | bytes 262176 | tf_op jit(solution)/shard_map/ppermute | solution.py:46
  268.7 1.7 constant_dynamic-update-slice_fusion.3
  270.4 0.7 constant_dynamic-update-slice_fusion.2
  271.0 0.7 constant_dynamic-update-slice_fusion.1
  271.7 1.7 constant_dynamic-update-slice_fusion
  273.4 92.1 %reduce-scatter.3.cloned.1.call-done = f32[192,2,2048]{2,0,1:T(8,128)} async-done(((f32[768,2,2048]{2,0,1:T(8,128)}), f32[192,2,2048]{2,0,1:T(8,128)}) %reduce-scatter.3.cloned.1.call-update) | async-done | bytes 3145744 | tf_op jit(solution)/shard_map/reduce_scatter | solution.py:52
  365.5 0.0 copy-done.6
  365.5 0.0 copy-start.4
  365.5 4.9 %bitcast_add_fusion = f32[2,192,2048]{2,1,0:T(8,128)S(1)} fusion(f32[192,2,2048]{2,0,1:T(8,128)} %reduce-scatter.3.cloned.1.call-done, f32[2,192,32]{1,2,0:T(8,128)S(1)} %copy-done.6, f32[2,32,4096]{2,1,0:T(8,128)} %constant_dynamic-update-slice_fusion, s32[]{:T(128)S(6)} %select_n.28), kind=kOutput, calls=%fused_computation.8 | convolution fusion | flops 303562752 | bytes 6864900 | tf_op jit(solution)/shard_map/efr,erd->efd/dot_general | solution.py:61
  370.4 0.0 copy-start.1
  370.4 1.7 copy-done.1
  372.1 0.0 copy-done.4
  372.1 3.1 fusion.16
  375.2 0.2 fusion.17
  375.4 15.9 %psum.7 = f32[2,32,32]{1,2,0:T(8,128)S(1)} all-reduce(f32[2,32,32]{1,2,0:T(8,128)S(1)} %fusion.17), channel_id=1, replica_groups=mesh['expert'=64,'zero'=4] {'zero'}, use_global_device_ids=true, to_apply=%region_5.6 | all-reduce | flops 2048 | bytes 16384 | tf_op jit(solution)/shard_map/psum | solution.py:21
  391.3 0.1 copy.35
  391.4 5.9 %custom-call.7 = f32[2,32,32]{2,1,0:T(8,128)S(1)} custom-call(f32[2,32,32]{2,1,0:T(8,128)S(1)} %fusion.14), custom_call_target="Cholesky" | custom-call | tf_op jit(solution)/shard_map/jit(cholesky)/cholesky | solution.py:22
  397.3 0.1 compare_reduce_fusion
  397.4 0.1 select_bitcast_fusion
  397.5 4.9 %custom-call.8 = f32[2,1,32,32]{2,3,1,0:T(8,128)S(1)} custom-call(f32[2,1,32,32]{3,2,1,0:T(8,128)S(1)} %select_bitcast_fusion), custom_call_target="InvertDiagBlocksLowerTriangular" | custom-call | tf_op jit(solution)/shard_map/triangular_solve | solution.py:23
  402.4 0.3 fusion.12
  402.7 0.0 copy-start.5
  402.7 4.7 %convolution_multiply_fusion = f32[2,32,2048]{2,1,0:T(8,128)} fusion(f32[2,32,192]{2,1,0:T(8,128)S(1)} %fusion.12, f32[2,192,2048]{2,1,0:T(8,128)} %copy-done.1), kind=kOutput, calls=%fused_computation.9 | convolution fusion | flops 302120960 | bytes 3719168 | tf_op jit(solution)/shard_map/efr,efd->erd/dot_general | solution.py:66
  407.4 0.0 reduce-scatter.5.cloned.1.call-update
  407.4 22.4 %reduce-scatter.5.cloned.1.call-done = f32[2,32,512]{2,1,0:T(8,128)} async-done(((f32[2,32,2048]{2,1,0:T(8,128)}), f32[2,32,512]{2,1,0:T(8,128)}) %reduce-scatter.5.cloned.1.call-update) | async-done | bytes 131088 | tf_op jit(solution)/shard_map/reduce_scatter | solution.py:67
  429.8 0.0 copy-done.5
  (9 shorter events, 0.1 us)
Async XLA Ops:
  7.2 227.6 %copy-start = (bf16[2,1024,768]{2,1,0:T(8,128)(2,1)S(1)}, bf16[2,1024,768]{2,1,0:T(8,128)(2,1)}, u32[]{:S(2)}) copy-start(bf16[2,1024,768]{2,1,0:T(8,128)(2,1)} %param.10) | copy-start | bytes 9437188
  7.2 7.5 %copy-start.7 = (f32[128,8]{0,1:T(8,128)S(1)}, f32[128,8]{0,1:T(8,128)}, u32[]{:S(2)}) copy-start(f32[128,8]{0,1:T(8,128)} %param.8) | copy-start | bytes 12292
  7.2 358.3 %reduce-scatter.3.cloned.1.call-start = ((), (), s32[]{:S(2)}) async-start(), calls=%async_computation.3 | async-start | bytes 15728640 | tf_op jit(solution)/shard_map/reduce_scatter | solution.py:52
  9.6 0.8 copy-start.2
  247.4 0.9 copy-start.3
  247.4 118.1 %copy-start.6 = (f32[2,192,32]{1,2,0:T(8,128)S(1)}, f32[2,192,32]{1,2,0:T(8,128)}, u32[]{:S(2)}) copy-start(f32[2,192,32]{1,2,0:T(8,128)} %param.11) | copy-start | bytes 147460
  247.4 182.4 %reduce-scatter.5.cloned.1.call-start = ((), (), s32[]{:S(2)}) async-start(), calls=%async_computation.4 | async-start | bytes 655360 | tf_op jit(solution)/shard_map/reduce_scatter | solution.py:67
  248.3 5.5 %collective-permute-start = (f32[2,32,512]{2,1,0:T(8,128)S(1)}, f32[2,32,512]{2,1,0:T(8,128)S(1)}, u32[]{:S(2)}, u32[]{:S(2)}) collective-permute-start(f32[2,32,512]{2,1,0:T(8,128)S(1)} %copy-done.3), channel_id=1, source_target_pairs={{0,3},{1,0},{2,1},{3,2},{4,7},{5,4},{6,5},{7,6},{8,11},{9,8},{10,9... | collective-permute-start | bytes 393224 | tf_op jit(solution)/shard_map/ppermute | solution.py:46
  254.5 14.2 %collective-permute-start.1 = (f32[2,32,1024]{2,1,0:T(8,128)}, f32[2,32,1024]{2,1,0:T(8,128)}, u32[]{:S(2)}, u32[]{:S(2)}) collective-permute-start(f32[2,32,1024]{2,1,0:T(8,128)} %pad_maximum_fusion), channel_id=1, source_target_pairs={{0,2},{1,3},{2,0},{3,1},{4,6},{5,7},{6,4},{7,5},{8,10},{9,11},{10,... | collective-permute-start | bytes 786440 | tf_op jit(solution)/shard_map/ppermute | solution.py:46
  365.5 6.6 %copy-start.4 = (f32[2,2048,32]{1,2,0:T(8,128)S(1)}, f32[2,2048,32]{1,2,0:T(8,128)}, u32[]{:S(2)}) copy-start(f32[2,2048,32]{1,2,0:T(8,128)} %param.13) | copy-start | bytes 1572868
  370.4 1.7 copy-start.1
  402.7 27.1 %copy-start.5 = (f32[2,32,192]{2,1,0:T(8,128)}, f32[2,32,192]{2,1,0:T(8,128)S(1)}, u32[]{:S(2)}) copy-start(f32[2,32,192]{2,1,0:T(8,128)S(1)} %fusion.12) | copy-start | bytes 147460
Sparse Core Ops, SparseCore 0:
  247.5 117.9 reduce-scatter.2
  407.5 22.1 reduce-scatter.4
